TPU v7x, 128 devices: a whole 4x4x4 slice. The times are simulated.
128 devices in a mesh: batch: 4 (over z), seq: 32 (over y, x, core).
Axes of the slice: x: 4, y: 4, z: 4, core: 2. Of those that a mesh axis runs over, the one named last changes fastest.
Arguments:
- packed: bfloat16 [131072, 768], P(('batch', 'seq')), may hold values from -5 to 5
- block_dest: int32 [4096], P(('batch', 'seq')), may hold values from 0 to 1023, as said below
- doc_len: int32 [20], P('batch'), may hold values from 6400 to 8192, as said below
- w_qkv: bfloat16 [768, 2304], replicated
- b_qkv: float32 [2304], replicated, may hold values from -3 to 3
- w_out: bfloat16 [768, 768], replicated, may hold values from -0.21875 to 0.21875
- b_out: float32 [768], replicated, may hold values from -3 to 3
- norm1_gain: float32 [768], replicated, may hold values from 0.1 to 1.9
- norm1_shift: float32 [768], replicated, may hold values from -2 to 2
- w_glu: bfloat16 [768, 6144], replicated, may hold values from -0.21875 to 0.21875
- w_down: bfloat16 [3072, 768], replicated, may hold values from -0.109375 to 0.109375
- b_down: float32 [768], replicated, may hold values from -3 to 3
- norm2_gain: float32 [768], replicated, may hold values from 0.1 to 1.9
- norm2_shift: float32 [768], replicated, may hold values from -2 to 2
- centroids: bfloat16 [256, 768], replicated, may hold values from -3 to 3
- tile_list: int32 [512], P(('batch', 'seq')), may hold values from 0 to 255, as said below
Outputs:
- encoded: bfloat16 [131072, 768], P(('batch', 'seq'))
- stored: bfloat16 [4, 32, 1024, 768], P('batch', 'seq')
Inputs may be any that keep to these rules, and one draw needn't show every extreme that they name: `block_dest`: within a group, the entries of its 32 devices form a permutation of the group's block positions; position q is block q % 32 of sequence shard q // 32. At most 2 blocks of one device go to one shard. `doc_len`: valid tokens counted from the document's start in the stream. `tile_list`: list // 64 is the batch index that owns the list; at most 2 tiles of one device share an owner.
All inputs are finite; a program needn't handle non-finite values.
Results may differ from a plain program's by a relative error of at most 0.011.
Values may be sent and summed in bfloat16 or wider, within the bound.
No kernel may reach another device: no remote copies, remote signals or barrier semaphores. Data moves between devices by JAX's collectives and lax.ppermute only.
A program may use at most 192 MiB of HBM per device.

v0:
```python
import functools
import math

import jax
import jax.numpy as jnp
import numpy as np
from jax import lax
from jax.experimental import pallas as pl
from jax.experimental.pallas import tpu as pltpu
from jax.sharding import PartitionSpec as P

H = 12
D = 768
FF = 3072
DOC_LEN = 8192
BAND = 256
CAP = 2
TROWS = 128
LPO = 64
NSEQ = 32
SDEV = 1024
BLK = 32
LEAD = 512
SPAN = NSEQ * SDEV
CH = 256
WIN = CH + 2 * BAND
FC = 256

norm_eps = 1e-06
LOG2E = math.log2(math.e)
FAR = -1e32
MIB = 1 << 20

ANY = pl.BlockSpec(memory_space=pl.ANY)
VMEM = pl.BlockSpec(memory_space=pltpu.VMEM)
SMEM = pl.BlockSpec(memory_space=pltpu.SMEM)
F32 = jnp.float32
BF16 = jnp.bfloat16


def head_slopes(heads):
    base = 2 ** int(np.floor(np.log2(heads)))
    first = [2.0 ** (-8.0 * (i + 1) / base) for i in range(base)]
    extra = [2.0 ** (-4.0 * (i + 1) / base) for i in range(2 * (heads - base))][0::2]
    return np.asarray(first + extra, np.float32)


def iota(shape, dim):
    return lax.broadcasted_iota(jnp.int32, shape, dim)


def dot(a, b):
    return jnp.dot(a, b, preferred_element_type=F32)


def pack_kernel(dest, packed, buffer, count, sems):
    def clear(i, _):
        count[i] = 0
        return 0

    lax.fori_loop(0, NSEQ, clear, 0)

    def copy_of(j, slot):
        return pltpu.make_async_copy(
            packed.at[pl.ds(pl.multiple_of(j * BLK, BLK), BLK)], buffer.at[slot], sems.at[j]
        )

    def send(j, _):
        owner = lax.shift_right_logical(dest[j], 5)
        rank = count[owner]
        count[owner] = rank + 1
        copy_of(j, owner * CAP + rank).start()
        return 0

    lax.fori_loop(0, BLK, send, 0)

    def finish(j, _):
        copy_of(j, 0).wait()
        return 0

    lax.fori_loop(0, BLK, finish, 0)


def pack(packed, dest):
    return pl.pallas_call(
        pack_kernel,
        out_shape=jax.ShapeDtypeStruct((NSEQ * CAP, BLK, D), BF16),
        in_specs=[SMEM, ANY],
        out_specs=ANY,
        scratch_shapes=[pltpu.SMEM((NSEQ,), jnp.int32), pltpu.SemaphoreType.DMA((BLK,))],
        name="pack_blocks",
    )(dest, packed)


def edge_kernel(src, received, head, tail, sems):
    copies = []
    per = BAND // BLK
    for q in range(per):
        copies.append(
            pltpu.make_async_copy(
                received.at[src[q]], head.at[pl.ds(q * BLK, BLK)], sems.at[q]
            )
        )
        copies.append(
            pltpu.make_async_copy(
                received.at[src[SDEV // BLK - per + q]],
                tail.at[pl.ds(q * BLK, BLK)],
                sems.at[per + q],
            )
        )
    for c in copies:
        c.start()
    for c in copies:
        c.wait()


def edges(src, received):
    shape = jax.ShapeDtypeStruct((BAND, D), BF16)
    return pl.pallas_call(
        edge_kernel,
        out_shape=(shape, shape),
        in_specs=[SMEM, ANY],
        out_specs=(ANY, ANY),
        scratch_shapes=[pltpu.SemaphoreType.DMA((2 * BAND // BLK,))],
        name="shard_edges",
    )(src, received)


def doc_bounds(info, doc_len, start):
    u0 = info[0] + LEAD + start
    doc = lax.shift_right_logical(u0, 13)
    base = doc * DOC_LEN
    length = doc_len[doc]
    low = jnp.maximum(0, LEAD - base)
    high = jnp.minimum(length, SPAN + LEAD - base)
    return u0 - base, length, low, high


def reach_table(info, doc_len, start):
    rel, _, low, high = doc_bounds(info, doc_len, start)
    j = iota((CH, WIN), 1)
    dist = jnp.abs(iota((CH, WIN), 0) + BAND - j)
    key = rel - BAND + j
    keep = (dist <= BAND) & (((key >= low) & (key < high)) | (dist == 0))
    return jnp.where(keep, -dist.astype(F32), FAR)


def layer_norm(v, gain, shift):
    centre = jnp.mean(v, axis=-1, keepdims=True)
    v = v - centre
    spread = jnp.mean(v * v, axis=-1, keepdims=True)
    return v * lax.rsqrt(spread + norm_eps) * gain + shift


def gelu(x):
    z = jnp.abs(x)
    t = 1.0 / (1.0 + z * (0.3275911 * math.sqrt(0.5)))
    p = t * (0.5 * 1.061405429) + (0.5 * -1.453152027)
    p = p * t + (0.5 * 1.421413741)
    p = p * t + (0.5 * -0.284496736)
    p = p * t + (0.5 * 0.254829592)
    q = p * t * jnp.exp2(x * x * (-0.5 * LOG2E))
    return jnp.maximum(x, 0.0) - z * q


def attend_pair(pair, chunks, qref, qrows, kvref, reach, slopes, att):
    lanes = pl.ds(pl.multiple_of(pair * 128, 128), 128)
    vlanes = pl.ds(pl.multiple_of(D + pair * 128, 128), 128)
    left = iota((CH, 128), 1) < 64
    ones = jnp.ones((WIN, 128), BF16)
    for n, c in enumerate(chunks):
        q = qref[pl.ds(qrows[n], CH), lanes]
        window = pl.ds(c * CH - kvref[1], WIN)
        k = kvref[0][window, lanes]
        v = jnp.concatenate([kvref[0][window, vlanes], ones], axis=1)
        halves = []
        for side in range(2):
            mine = left if side == 0 else jnp.logical_not(left)
            s = lax.dot_general(
                jnp.where(mine, q, jnp.zeros_like(q)),
                k,
                (((1,), (1,)), ((), ())),
                preferred_element_type=F32,
            )
            s = s + slopes[2 * pair + side] * reach[n]
            s = s - jnp.max(s, axis=-1, keepdims=True)
            o = dot(jnp.exp2(s).astype(BF16), v)
            halves.append(o[:, :128] / o[:, 128:])
        att[pl.ds(n * CH, CH), lanes] = jnp.where(left, halves[0], halves[1]).astype(BF16)


def tail_of_layer(chunks, x_of, att, first, active, w_out, w_glu, w_down, vecs, waits):
    b_out, g1, s1, b_down, g2, s2 = vecs
    rows = len(chunks) * CH
    waits[0]()
    mixed = dot(att[...], w_out[...]) + b_out[...] + x_of().astype(F32)
    first[...] = layer_norm(mixed, g1[...], s1[...]).astype(BF16)
    waits[1]()

    def part(i, _):
        cols = pl.ds(pl.multiple_of(i * FC, FC), FC)
        up = pl.ds(pl.multiple_of(FF + i * FC, FC), FC)
        f = first[...]
        active[:, cols] = (gelu(dot(f, w_glu[:, cols])) * dot(f, w_glu[:, up])).astype(BF16)
        return 0

    lax.fori_loop(0, FF // FC, part, 0)
    waits[2]()
    second = dot(active[...], w_down[...]) + b_down[...] + first[...].astype(F32)
    return layer_norm(second, g2[...], s2[...]).astype(BF16)


def pool_tile(info, doc_len, lists, chunk, enc, centroids):
    rel, length, _, _ = doc_bounds(info, doc_len, chunk * CH)
    r = iota((TROWS, CH), 0)
    i = iota((TROWS, CH), 1)
    scale = jnp.where(length - rel - 2 * r >= 2, 0.5, 1.0)
    mine = (lax.shift_right_logical(i, 1) == r) & (rel + i < length)
    pooled = dot(jnp.where(mine, scale, 0.0).astype(BF16), enc)
    pick = (iota((TROWS, centroids.shape[0]), 1) == lists[chunk]).astype(BF16)
    return (pooled - dot(pick, centroids[...])).astype(BF16)


def start_all(copies):
    for c in copies:
        c.start()


def mid_kernel(
    src, info, doc_len, lists, slopes,
    received, w_qkv_h, w_out_h, w_glu_h, w_down_h,
    b_qkv, b_out, g1, s1, b_down, g2, s2, centroids,
    enc_h, q_h, kv_h, tiles,
    x, w_qkv, w_out, w_glu, w_down, qs, kvs, att, first, active, reach, enc, wsem, xsem, osem,
):
    weights = [
        pltpu.make_async_copy(h, v, wsem.at[i])
        for i, (h, v) in enumerate(
            [(w_qkv_h, w_qkv), (w_out_h, w_out), (w_glu_h, w_glu), (w_down_h, w_down)]
        )
    ]
    blocks = [
        pltpu.make_async_copy(received.at[src[q]], x.at[pl.ds(q * BLK, BLK)], xsem.at[q])
        for q in range(SDEV // BLK)
    ]
    start_all(blocks)
    start_all(weights)
    chunks = (1, 2)
    for n, c in enumerate(chunks):
        reach[n] = reach_table(info, doc_len, c * CH)
    for b in blocks:
        b.wait()
    weights[0].wait()
    qs[...] = ((dot(x[...], w_qkv[:, :D]) + b_qkv[:, :D]) * (LOG2E / 8.0)).astype(BF16)
    kvs[...] = (dot(x[...], w_qkv[:, D:]) + b_qkv[:, D:]).astype(BF16)
    outs = [
        pltpu.make_async_copy(qs, q_h, osem.at[0]),
        pltpu.make_async_copy(kvs, kv_h, osem.at[1]),
    ]
    start_all(outs)

    def pairs(pair, _):
        attend_pair(pair, chunks, qs, (CH, 2 * CH), (kvs, BAND), reach, slopes, att)
        return 0

    lax.fori_loop(0, H // 2, pairs, 0)
    enc[...] = tail_of_layer(
        chunks, lambda: x[pl.ds(CH, 2 * CH)], att, first, active, w_out, w_glu, w_down,
        (b_out, g1, s1, b_down, g2, s2), [w.wait for w in weights[1:]],
    )
    last = pltpu.make_async_copy(enc, enc_h.at[pl.ds(CH, 2 * CH)], osem.at[2])
    last.start()
    for n, c in enumerate(chunks):
        tiles[n] = pool_tile(info, doc_len, lists, c, enc[pl.ds(n * CH, CH)], centroids)
    for o in outs + [last]:
        o.wait()


def edge_layer_kernel(
    src, info, doc_len, lists, slopes,
    received, before, after, q_h, kv_h, enc_in, w_qkv_h, w_out_h, w_glu_h, w_down_h,
    b_qkv, b_out, g1, s1, b_down, g2, s2, centroids,
    enc_h, tiles,
    x, halo, w_kv, w_out, w_glu, w_down, qs, kvs, att, first, active, reach, enc, wsem, xsem, osem,
):
    weights = [
        pltpu.make_async_copy(h, v, wsem.at[i])
        for i, (h, v) in enumerate(
            [
                (w_qkv_h.at[:, pl.ds(D, 2 * D)], w_kv),
                (w_out_h, w_out),
                (w_glu_h, w_glu),
                (w_down_h, w_down),
            ]
        )
    ]
    per = CH // BLK
    total = SDEV // BLK
    blocks = [
        pltpu.make_async_copy(
            received.at[src[q if q < per else total - 2 * per + q]],
            x.at[pl.ds(q * BLK, BLK)],
            xsem.at[q],
        )
        for q in range(2 * per)
    ]
    loads = [
        pltpu.make_async_copy(before, halo.at[pl.ds(0, BAND)], osem.at[0]),
        pltpu.make_async_copy(after, halo.at[pl.ds(BAND, BAND)], osem.at[1]),
    ]
    own = [
        pltpu.make_async_copy(q_h.at[pl.ds(0, CH)], qs.at[pl.ds(0, CH)], osem.at[2]),
        pltpu.make_async_copy(q_h.at[pl.ds(SDEV - CH, CH)], qs.at[pl.ds(CH, CH)], osem.at[3]),
        pltpu.make_async_copy(kv_h, kvs.at[pl.ds(BAND, SDEV)], osem.at[4]),
    ]
    start_all(loads)
    weights[0].start()
    start_all(own)
    start_all(blocks)
    start_all(weights[1:])
    chunks = (0, 3)
    for n, c in enumerate(chunks):
        reach[n] = reach_table(info, doc_len, c * CH)
    for c in loads:
        c.wait()
    weights[0].wait()
    sides = (dot(halo[...], w_kv[...]) + b_qkv[:, D:]).astype(BF16)
    kvs[pl.ds(0, BAND)] = sides[:BAND]
    kvs[pl.ds(BAND + SDEV, BAND)] = sides[BAND:]
    for c in own:
        c.wait()

    def pairs(pair, _):
        attend_pair(pair, chunks, qs, (0, CH), (kvs, 0), reach, slopes, att)
        return 0

    lax.fori_loop(0, H // 2, pairs, 0)
    for b in blocks:
        b.wait()
    enc[...] = tail_of_layer(
        chunks, lambda: x[...], att, first, active, w_out, w_glu, w_down,
        (b_out, g1, s1, b_down, g2, s2), [w.wait for w in weights[1:]],
    )
    last = [
        pltpu.make_async_copy(enc.at[pl.ds(0, CH)], enc_h.at[pl.ds(0, CH)], osem.at[5]),
        pltpu.make_async_copy(enc.at[pl.ds(CH, CH)], enc_h.at[pl.ds(SDEV - CH, CH)], osem.at[6]),
    ]
    start_all(last)
    for n, c in enumerate(chunks):
        tiles[n] = pool_tile(info, doc_len, lists, c, enc[pl.ds(n * CH, CH)], centroids)
    for o in last:
        o.wait()


def dma(*shape):
    return pltpu.SemaphoreType.DMA(shape)


def common_scratch():
    return [
        pltpu.VMEM((2 * CH, D), BF16),
        pltpu.VMEM((2 * CH, D), BF16),
        pltpu.VMEM((2 * CH, FF), BF16),
        pltpu.VMEM((2, CH, WIN), F32),
        pltpu.VMEM((2 * CH, D), BF16),
    ]


def mid_layer(src, info, doc_len, lists, slopes, received, ws, vecs):
    return pl.pallas_call(
        mid_kernel,
        out_shape=(
            jax.ShapeDtypeStruct((SDEV, D), BF16),
            jax.ShapeDtypeStruct((SDEV, D), BF16),
            jax.ShapeDtypeStruct((SDEV, 2 * D), BF16),
            jax.ShapeDtypeStruct((2, TROWS, D), BF16),
        ),
        in_specs=[SMEM] * 5 + [ANY] * 5 + [VMEM] * 8,
        out_specs=(ANY, ANY, ANY, VMEM),
        scratch_shapes=[
            pltpu.VMEM((SDEV, D), BF16),
            pltpu.VMEM((D, 3 * D), BF16),
            pltpu.VMEM((D, D), BF16),
            pltpu.VMEM((D, 2 * FF), BF16),
            pltpu.VMEM((FF, D), BF16),
            pltpu.VMEM((SDEV, D), BF16),
            pltpu.VMEM((SDEV, 2 * D), BF16),
        ]
        + common_scratch()
        + [dma(4), dma(SDEV // BLK), dma(3)],
        compiler_params=pltpu.CompilerParams(vmem_limit_bytes=56 * MIB),
        cost_estimate=pl.CostEstimate(
            flops=14_000_000_000, bytes_accessed=30_000_000, transcendentals=8_000_000
        ),
        name="mid_layer",
    )(src, info, doc_len, lists, slopes, received, *ws, *vecs)


def edge_layer(src, info, doc_len, lists, slopes, received, before, after, q, kv, enc, ws, vecs):
    return pl.pallas_call(
        edge_layer_kernel,
        out_shape=(
            jax.ShapeDtypeStruct((SDEV, D), BF16),
            jax.ShapeDtypeStruct((2, TROWS, D), BF16),
        ),
        in_specs=[SMEM] * 5 + [ANY] * 10 + [VMEM] * 8,
        out_specs=(ANY, VMEM),
        input_output_aliases={10: 0},
        scratch_shapes=[
            pltpu.VMEM((2 * CH, D), BF16),
            pltpu.VMEM((2 * BAND, D), BF16),
            pltpu.VMEM((D, 2 * D), BF16),
            pltpu.VMEM((D, D), BF16),
            pltpu.VMEM((D, 2 * FF), BF16),
            pltpu.VMEM((FF, D), BF16),
            pltpu.VMEM((2 * CH, D), BF16),
            pltpu.VMEM((SDEV + 2 * BAND, 2 * D), BF16),
        ]
        + common_scratch()
        + [dma(4), dma(2 * CH // BLK), dma(7)],
        compiler_params=pltpu.CompilerParams(vmem_limit_bytes=56 * MIB),
        cost_estimate=pl.CostEstimate(
            flops=12_000_000_000, bytes_accessed=30_000_000, transcendentals=8_000_000
        ),
        name="edge_layer",
    )(src, info, doc_len, lists, slopes, received, before, after, q, kv, enc, *ws, *vecs)


def store_kernel(pick, a, b, zeros, out, sems):
    copies = []
    for slot in range(8):
        dst = out.at[pl.ds(slot * TROWS, TROWS)]
        code = pick[slot]
        which = jnp.maximum(code, 0)

        @pl.when(code < 0)
        def _():
            pltpu.make_async_copy(zeros, dst, sems.at[slot]).start()

        @pl.when((code >= 0) & (lax.rem(which, 4) < 2))
        def _():
            n = lax.div(which, 4) * 2 + lax.rem(which, 4)
            pltpu.make_async_copy(a.at[n], dst, sems.at[slot]).start()

        @pl.when((code >= 0) & (lax.rem(which, 4) >= 2))
        def _():
            n = lax.div(which, 4) * 2 + lax.rem(which, 4) - 2
            pltpu.make_async_copy(b.at[n], dst, sems.at[slot]).start()

        copies.append(pltpu.make_async_copy(zeros, dst, sems.at[slot]))
    for c in copies:
        c.wait()


def store(pick, a, b):
    return pl.pallas_call(
        store_kernel,
        out_shape=jax.ShapeDtypeStruct((8 * TROWS, D), BF16),
        in_specs=[SMEM, ANY, ANY, VMEM],
        out_specs=ANY,
        scratch_shapes=[dma(8)],
        name="store_tiles",
    )(pick, a, b, jnp.zeros((TROWS, D), BF16))


def arrival_slots(dests, me):
    mine = (dests // NSEQ) == me
    order = jnp.arange(BLK, dtype=jnp.int32)
    before = (order[:, None] < order[None, :]).astype(F32)
    rank = jnp.dot(mine.astype(F32), before).astype(jnp.int32)
    slot = jnp.arange(NSEQ, dtype=jnp.int32)[:, None] * CAP + rank
    place = jnp.where(mine, dests % NSEQ, -1).reshape(1, -1)
    hit = place == jnp.arange(NSEQ, dtype=jnp.int32)[:, None]
    return jnp.sum(jnp.where(hit, slot.reshape(1, -1), 0), axis=1)


def stored_slots(lists, me):
    owner = lists // LPO
    mine = owner == me
    order = jnp.arange(4, dtype=jnp.int32)
    rank = jnp.sum(
        (mine[:, None, :] & (order[None, None, :] < order[None, :, None])).astype(jnp.int32), axis=2
    )
    place = jnp.asarray([2, 0, 1, 3], jnp.int32)
    code = jnp.arange(4, dtype=jnp.int32)[:, None] * 4 + place[None, :]
    slots = jnp.arange(2, dtype=jnp.int32)
    hit = mine[:, None, :] & (rank[:, None, :] == slots[None, :, None])
    return (jnp.sum(jnp.where(hit, code[:, None, :] + 1, 0), axis=2) - 1).reshape(-1)


def on_device(
    packed, block_dest, doc_len, w_qkv, b_qkv, w_out, b_out, norm1_gain, norm1_shift,
    w_glu, w_down, b_down, norm2_gain, norm2_shift, centroids, tile_list,
):
    seq_here = lax.axis_index("seq")
    batch_here = lax.axis_index("batch")
    dests = lax.all_gather(block_dest, "seq", axis=0)
    lists = lax.all_gather(tile_list, "batch", axis=0)
    received = lax.all_to_all(
        pack(packed, block_dest), "seq", split_axis=0, concat_axis=0, tiled=True
    )
    src = arrival_slots(dests, seq_here)
    pick = stored_slots(lists, batch_here)
    info = (seq_here * SDEV).astype(jnp.int32).reshape(1)
    slopes = jnp.asarray(head_slopes(H) * np.float32(LOG2E))
    row = lambda v: v.reshape(1, -1)
    ws = (w_qkv, w_out, w_glu, w_down)
    vecs = (
        row(b_qkv), row(b_out), row(norm1_gain), row(norm1_shift),
        row(b_down), row(norm2_gain), row(norm2_shift), centroids,
    )
    head, tail = edges(src, received)
    up = [(i, i + 1) for i in range(NSEQ - 1)]
    down = [(j, i) for i, j in up]
    before = lax.ppermute(tail, "seq", up)
    after = lax.ppermute(head, "seq", down)
    enc, q, kv, tiles_a = mid_layer(src, info, doc_len, tile_list, slopes, received, ws, vecs)
    all_a = lax.all_gather(tiles_a, "batch", axis=0, tiled=True)
    enc, tiles_b = edge_layer(
        src, info, doc_len, tile_list, slopes, received, before, after, q, kv, enc, ws, vecs
    )
    all_b = lax.all_gather(tiles_b, "batch", axis=0, tiled=True)
    stored = store(pick, all_a, all_b)
    return enc, stored.reshape(1, 1, 8 * TROWS, D)


def solution(mesh):
    return jax.shard_map(
        on_device,
        mesh=mesh,
        in_specs=(
            P(("batch", "seq"), None),
            P(("batch", "seq")),
            P("batch"),
            P(), P(), P(), P(), P(), P(), P(), P(), P(), P(), P(), P(),
            P(("batch", "seq")),
        ),
        out_specs=(P(("batch", "seq"), None), P("batch", "seq", None, None)),
        check_vma=False,
    )
```

profile of v0, /device:TPU:18, one launch (start us, length us, event | category | flops | bytes accessed | tf_op | source)
XLA Modules:
  0.0 316.6 jit_solution(5195815751416043859)
XLA Ops:
  7.2 49.9 %pack_blocks.1 = bf16[64,32,768]{2,1,0:T(8,128)(2,1)} custom-call(s32[32]{0:T(128)} %dest.1, bf16[1024,768]{1,0:T(8,128)(2,1)} %packed.1), custom_call_target="tpu_custom_call" | custom-call | tf_op jit(solution)/shard_map/pack_blocks/pallas_call | solution.py:85
  57.1 0.0 copy-start.14
  57.1 0.0 copy-start.8
  57.1 0.0 copy-start.1
  57.1 0.0 copy-start.3
  57.1 0.0 copy-start.4
  57.2 0.0 copy-start.7
  57.2 7.5 %all-to-all-start = ((bf16[64,32,768]{2,1,0:T(8,128)(2,1)}), bf16[64,32,768]{2,1,0:T(8,128)(2,1)S(1)}, u32[]{:S(2)}, u32[]{:S(2)}) async-start(bf16[64,32,768]{2,1,0:T(8,128)(2,1)} %pack_blocks.1), calls=%async_computation | async-start | bytes 6291456 | tf_op jit(solution)/shard_map/all_to_all | solution.py:499
  64.7 0.0 all-gather.5.cloned.1.call-start
  64.8 0.6 dynamic-slice
  66.1 0.2 dynamic-update-slice
  66.3 45.3 %all-reduce = s32[1024]{0:T(1024)S(1)} all-reduce(s32[1024]{0:T(1024)S(1)} %dynamic-update-slice), channel_id=2, replica_groups=mesh['batch'=4,'seq'=32] {'seq'}, use_global_device_ids=true, to_apply=%add | all-reduce | flops 1024 | bytes 8192
  111.6 0.1 reshape.100
  111.7 0.1 fusion
  111.8 0.1 broadcast_in_dim.26
  111.9 0.1 eq.44
  112.0 0.6 reshape.92.b_qkv
  112.6 0.6 reshape.93.b_out
  113.2 0.6 reshape.94.g1
  113.8 0.6 reshape.95.s1
  114.4 0.6 reshape.96.b_down
  115.0 0.6 reshape.97.g2
  115.6 0.6 reshape.98.s2
  116.2 0.6 select_reduce_fusion.src
  116.8 1.6 copy-done
  118.5 37.6 %mid_layer.1 = (bf16[1024,768]{1,0:T(8,128)(2,1)}, bf16[1024,768]{1,0:T(8,128)(2,1)}, bf16[1024,1536]{1,0:T(8,128)(2,1)}, bf16[2,128,768]{2,1,0:T(8,128)(2,1)}) custom-call(s32[32]{0:T(128)} %select_reduce_fusion.src, s32[1]{0:T(128)} %bitcast.1.info, s32[5]{0:T(128)} %doc_len.3, s32[4]{0:T(128)} %lists.3, f32[12]{0:T(128)} %constant.68.clone.slopes, ...), custom_call_target="tpu_custom_call" | custom-call | flops 14000000000 | bytes 30000000 | tf_op jit(solution)/shard_map/mid_layer/pallas_call | solution.py:370
  156.1 0.0 all-gather.5.cloned.1.call-update
  156.1 0.0 all-gather.7.cloned.1.call-start
  156.1 25.7 %shard_edges.1 = (bf16[256,768]{1,0:T(8,128)(2,1)}, bf16[256,768]{1,0:T(8,128)(2,1)}) custom-call(s32[32]{0:T(128)} %select_reduce_fusion.src, bf16[64,32,768]{2,1,0:T(8,128)(2,1)} %copy-done), custom_call_target="tpu_custom_call" | custom-call | tf_op jit(solution)/shard_map/shard_edges/pallas_call | solution.py:119
  181.9 1.9 collective-permute-start
  183.8 3.8 %collective-permute-start.1 = (bf16[256,768]{1,0:T(8,128)(2,1)}, bf16[256,768]{1,0:T(8,128)(2,1)S(1)}, u32[]{:S(2)}, u32[]{:S(2)}) collective-permute-start(bf16[256,768]{1,0:T(8,128)(2,1)} %get-tuple-element.11), channel_id=1, source_target_pairs={{1,0},{2,1},{3,2},{4,3},{5,4},{6,5},{7,6},{8,7},{9,8},{10,9},{11,1... | collective-permute-start | bytes 1179656 | tf_op jit(solution)/shard_map/ppermute | solution.py:516
  187.6 3.5 %collective-permute-done.before = bf16[256,768]{1,0:T(8,128)(2,1)S(1)} collective-permute-done((bf16[256,768]{1,0:T(8,128)(2,1)}, bf16[256,768]{1,0:T(8,128)(2,1)S(1)}, u32[]{:S(2)}, u32[]{:S(2)}) %collective-permute-start) | collective-permute-done | bytes 393248 | tf_op jit(solution)/shard_map/ppermute | solution.py:515
  191.2 1.9 collective-permute-done.1.after
  193.1 0.8 copy-done.11
  193.8 33.4 %edge_layer.1 = (bf16[1024,768]{1,0:T(8,128)(2,1)}, bf16[2,128,768]{2,1,0:T(8,128)(2,1)}) custom-call(s32[32]{0:T(128)} %select_reduce_fusion.src, s32[1]{0:T(128)} %bitcast.1.info, s32[5]{0:T(128)} %doc_len.3, s32[4]{0:T(128)} %lists.3, f32[12]{0:T(128)} %constant.68.clone.slopes, bf16[64,32,768]{2,1,0:T(8,128)(2,1)} %copy-done, ...), custom_call_target="tpu_custom_call", output_to_operand_aliasing={{0}: (10, {})} | custom-call | flops 12000000000 | bytes 30000000 | tf_op jit(solution)/shard_map/edge_layer/pallas_call | solution.py:400
  227.2 0.0 all-gather.7.cloned.1.call-update
  227.3 0.6 dynamic-slice.1
  228.5 0.2 dynamic-update-slice.1
  228.8 9.7 %all-reduce.1 = s32[16]{0:T(128)S(1)} all-reduce(s32[16]{0:T(128)S(1)} %dynamic-update-slice.1), channel_id=3, replica_groups=mesh['batch'=4,'seq'=32] {'batch'}, use_global_device_ids=true, to_apply=%add.1 | all-reduce | flops 16 | bytes 128
  238.5 0.1 reshape.101
  238.6 0.2 convert_reduce_fusion
  238.8 0.1 add_add_fusion
  238.8 0.1 select_reduce_fusion.1
  239.0 0.1 copy.21
  239.1 0.6 sub.18.pick
  239.7 19.6 %all-gather.7.cloned.1.call-done.b = bf16[8,128,768]{2,1,0:T(8,128)(2,1)} async-done(((bf16[2,128,768]{2,1,0:T(8,128)(2,1)}), bf16[8,128,768]{2,1,0:T(8,128)(2,1)}) %all-gather.7.cloned.1.call-update) | async-done | bytes 1572880 | tf_op jit(solution)/shard_map/all_gather | solution.py:522
  259.3 0.7 broadcast_in_dim.49.zeros
  260.0 49.8 %store_tiles.1 = bf16[1024,768]{1,0:T(8,128)(2,1)} custom-call(s32[8]{0:T(128)} %sub.18.pick, bf16[8,128,768]{2,1,0:T(8,128)(2,1)} %all-gather.5.cloned.1.call-done.a, bf16[8,128,768]{2,1,0:T(8,128)(2,1)} %all-gather.7.cloned.1.call-done.b, bf16[128,768]{1,0:T(8,128)(2,1)} %broadcast_in_dim.49.zeros), custom_call_target="tpu_custom_call" | custom-call | tf_op jit(solution)/shard_map/store_tiles/pallas_call | solution.py:456
  (32 shorter events, 0.1 us)
Async XLA Ops:
  57.1 7.7 %copy-start.14 = (u32[128]{0:T(128)S(1)}, u32[128]{0:T(128)}, u32[]{:S(2)}) copy-start(u32[128]{0:T(128)} %constant.74) | copy-start | bytes 1540
  57.1 9.0 %copy-start.8 = (s32[32]{0:T(128)S(1)}, s32[32]{0:T(128)}, u32[]{:S(2)}) copy-start(s32[32]{0:T(128)} %dest.1) | copy-start | bytes 388
  57.1 54.9 %copy-start.1 = (f32[2304]{0:T(1024)S(1)}, f32[2304]{0:T(1024)}, u32[]{:S(2)}) copy-start(f32[2304]{0:T(1024)} %param.22) | copy-start | bytes 27652
  57.1 55.5 %copy-start.2 = (f32[768]{0:T(1024)S(1)}, f32[768]{0:T(1024)}, u32[]{:S(2)}) copy-start(f32[768]{0:T(1024)} %param.24) | copy-start | bytes 9220
  57.1 56.1 %copy-start.3 = (f32[768]{0:T(1024)S(1)}, f32[768]{0:T(1024)}, u32[]{:S(2)}) copy-start(f32[768]{0:T(1024)} %param.25) | copy-start | bytes 9220
  57.1 56.7 %copy-start.4 = (f32[768]{0:T(1024)S(1)}, f32[768]{0:T(1024)}, u32[]{:S(2)}) copy-start(f32[768]{0:T(1024)} %param.26) | copy-start | bytes 9220
  57.1 57.2 %copy-start.5 = (f32[768]{0:T(1024)S(1)}, f32[768]{0:T(1024)}, u32[]{:S(2)}) copy-start(f32[768]{0:T(1024)} %param.29) | copy-start | bytes 9220
  57.2 57.8 %copy-start.6 = (f32[768]{0:T(1024)S(1)}, f32[768]{0:T(1024)}, u32[]{:S(2)}) copy-start(f32[768]{0:T(1024)} %param.30) | copy-start | bytes 9220
  57.2 58.4 %copy-start.7 = (f32[768]{0:T(1024)S(1)}, f32[768]{0:T(1024)}, u32[]{:S(2)}) copy-start(f32[768]{0:T(1024)} %param.31) | copy-start | bytes 9220
  57.2 59.6 %all-to-all-start = ((bf16[64,32,768]{2,1,0:T(8,128)(2,1)}), bf16[64,32,768]{2,1,0:T(8,128)(2,1)S(1)}, u32[]{:S(2)}, u32[]{:S(2)}) async-start(bf16[64,32,768]{2,1,0:T(8,128)(2,1)} %pack_blocks.1), calls=%async_computation | async-start | bytes 6291456 | tf_op jit(solution)/shard_map/all_to_all | solution.py:499
  64.7 175.0 %all-gather.5.cloned.1.call-start = ((), (), s32[]{:S(2)}) async-start(), calls=%async_computation.1 | async-start | bytes 1966080 | tf_op jit(solution)/shard_map/all_gather | solution.py:518
  116.8 1.6 copy-start
  156.1 103.2 %all-gather.7.cloned.1.call-start = ((), (), s32[]{:S(2)}) async-start(), calls=%async_computation.2 | async-start | bytes 1966080 | tf_op jit(solution)/shard_map/all_gather | solution.py:522
  181.9 9.3 %collective-permute-start = (bf16[256,768]{1,0:T(8,128)(2,1)}, bf16[256,768]{1,0:T(8,128)(2,1)S(1)}, u32[]{:S(2)}, u32[]{:S(2)}) collective-permute-start(bf16[256,768]{1,0:T(8,128)(2,1)} %get-tuple-element.10), channel_id=1, source_target_pairs={{0,1},{1,2},{2,3},{3,4},{4,5},{5,6},{6,7},{7,8},{8,9},{9,10},{10,1... | collective-permute-start | bytes 1179656 | tf_op jit(solution)/shard_map/ppermute | solution.py:515
  183.8 9.2 %collective-permute-start.1 = (bf16[256,768]{1,0:T(8,128)(2,1)}, bf16[256,768]{1,0:T(8,128)(2,1)S(1)}, u32[]{:S(2)}, u32[]{:S(2)}) collective-permute-start(bf16[256,768]{1,0:T(8,128)(2,1)} %get-tuple-element.11), channel_id=1, source_target_pairs={{1,0},{2,1},{3,2},{4,3},{5,4},{6,5},{7,6},{8,7},{9,8},{10,9},{11,1... | collective-permute-start | bytes 1179656 | tf_op jit(solution)/shard_map/ppermute | solution.py:516
  191.2 1.9 copy-start.10
  193.0 0.8 copy-start.11
  193.8 33.4 %copy-start.13 = (u32[128]{0:T(128)S(1)}, u32[128]{0:T(128)}, u32[]{:S(2)}) copy-start(u32[128]{0:T(128)} %constant.79) | copy-start | bytes 1540
  193.8 34.7 %copy-start.12 = (s32[4]{0:T(128)S(1)}, s32[4]{0:T(128)}, u32[]{:S(2)}) copy-start(s32[4]{0:T(128)} %lists.3) | copy-start | bytes 52
  193.8 44.9 %copy-start.9 = (s32[4]{0:T(128)S(1)}, s32[4]{0:T(128)}, u32[]{:S(2)}) copy-start(s32[4]{0:T(128)} %constant.67.clone) | copy-start | bytes 52
Sparse Core Ops, SparseCore 0:
  156.2 27.3 all-gather.4
  227.4 31.8 all-gather.6
where the time goes:
time: 316 us; the launch traced here: 317 us
  Pallas kernels  196 us (62%)
  blocking collectives  55 us (17%)
  waiting for transfers between devices  25 us (8%)
  between operations  15.6 us (5%)
  starting transfers between devices  13.4 us (4%)
  local copies, waits for them, and re-layouts  10.1 us (3%)
    unnamed x2, blocking collectives  55 us
    pallas_call x1, Pallas kernels, pack(): pl.pallas_call(pack_kernel, out_shape=jax.ShapeDtypeStruct((NSEQ * CAP, B...  49.9 us
    pallas_call x1, Pallas kernels, store(): pl.pallas_call(store_kernel, out_shape=jax.ShapeDtypeStruct((8 * TROWS, D...  49.8 us
    pallas_call x1, Pallas kernels, mid_layer(): pl.pallas_call(mid_kernel, out_shape=(jax.ShapeDtypeStruct((SDEV, D), BF1...  37.6 us
    pallas_call x1, Pallas kernels, edge_layer(): pl.pallas_call(edge_layer_kernel, out_shape=(jax.ShapeDtypeStruct((SDEV,...  33.4 us
    pallas_call x1, Pallas kernels, edges(): pl.pallas_call(edge_kernel, out_shape=(shape, shape), in_specs=[SMEM, ANY...  25.7 us
    all_gather x1, waiting for transfers between devices, on_device(): all_b = lax.all_gather(tiles_b, 'batch', axis=0, tiled=True)  19.6 us
    all_to_all x1, starting transfers between devices, on_device(): lax.all_to_all(pack(packed, block_dest), 'seq', split_axis=0, concat_axis...  7.55 us
  transfers between devices with their start and end apart: 5, of which 3 were waited for; matrix products, arithmetic and copies ran while one was open for 3% of the time, Pallas kernels for 19%

commit v1 on v0

v1 whole, which is shorter than its diff:
```python
import functools
import math

import jax
import jax.numpy as jnp
import numpy as np
from jax import lax
from jax.experimental import pallas as pl
from jax.experimental.pallas import tpu as pltpu
from jax.sharding import PartitionSpec as P

H = 12
D = 768
FF = 3072
DOC_LEN = 8192
BAND = 256
CAP = 2
TROWS = 128
LPO = 64
NSEQ = 32
BATCHES = 4
SDEV = 1024
BLK = 32
LEAD = 512
SPAN = NSEQ * SDEV
CH = 256
WIN = CH + 2 * BAND
GROUPS = D // 128
PIECES = CAP * GROUPS * BLK
LABEL_ROWS = 16
FC = 768
PAIR_UNROLL = 6
FF_UNROLL = 4

norm_eps = 1e-06
LOG2E = math.log2(math.e)
FAR = -1e32
MIB = 1 << 20
KERNEL_VMEM = 48 * MIB
SMALL_VMEM = 8 * MIB

ANY = pl.BlockSpec(memory_space=pl.ANY)
VMEM = pl.BlockSpec(memory_space=pltpu.VMEM)
SMEM = pl.BlockSpec(memory_space=pltpu.SMEM)
F32 = jnp.float32
BF16 = jnp.bfloat16


def head_slopes(heads):
    base = 2 ** int(np.floor(np.log2(heads)))
    first = [2.0 ** (-8.0 * (i + 1) / base) for i in range(base)]
    extra = [2.0 ** (-4.0 * (i + 1) / base) for i in range(2 * (heads - base))][0::2]
    return np.asarray(first + extra, np.float32)


def iota(shape, dim):
    return lax.broadcasted_iota(jnp.int32, shape, dim)


def dot(a, b):
    return jnp.dot(a, b, preferred_element_type=F32)


def piece(rank, group):
    return pl.ds(pl.multiple_of((rank * GROUPS + group) * BLK, BLK), BLK)


def pack_kernel(dest, packed, parts, count):
    def clear(i, _):
        count[i] = 0
        parts[i, pl.ds(PIECES, LABEL_ROWS)] = jnp.zeros((LABEL_ROWS, 128), BF16)
        return 0

    lax.fori_loop(0, NSEQ, clear, 0)
    lane = iota((LABEL_ROWS, 128), 1)

    def send(j, _):
        owner = lax.shift_right_logical(dest[j], 5)
        rank = count[owner]
        count[owner] = rank + 1
        rows = pl.ds(pl.multiple_of(j * BLK, BLK), BLK)
        for g in range(GROUPS):
            parts[owner, piece(rank, g)] = packed[rows, g * 128 : (g + 1) * 128]
        label = (dest[j] & (NSEQ - 1)) + 1
        old = parts[owner, pl.ds(PIECES, LABEL_ROWS)]
        new = jnp.where(lane == rank, label.astype(F32), old.astype(F32))
        parts[owner, pl.ds(PIECES, LABEL_ROWS)] = new.astype(BF16)
        return 0

    lax.fori_loop(0, BLK, send, 0)


def pack(packed, dest):
    return pl.pallas_call(
        pack_kernel,
        out_shape=jax.ShapeDtypeStruct((NSEQ, PIECES + LABEL_ROWS, 128), BF16),
        in_specs=[SMEM, VMEM],
        out_specs=VMEM,
        scratch_shapes=[pltpu.SMEM((NSEQ,), jnp.int32)],
        compiler_params=pltpu.CompilerParams(vmem_limit_bytes=SMALL_VMEM),
        name="pack_blocks",
    )(dest, packed)


def place_kernel(received, x, head, tail, vector, labels, sem):
    found = received[:, pl.ds(PIECES, LABEL_ROWS)].astype(F32)
    vector[...] = jnp.max(found, axis=1).astype(jnp.int32)
    copy = pltpu.make_async_copy(vector, labels, sem)
    copy.start()
    copy.wait()

    def fetch(source, _):
        for rank in range(CAP):
            label = labels[source, rank]

            @pl.when(label > 0)
            def _():
                rows = pl.ds(pl.multiple_of((label - 1) * BLK, BLK), BLK)
                for g in range(GROUPS):
                    x[rows, g * 128 : (g + 1) * 128] = received[source, piece(rank, g)]

        return 0

    lax.fori_loop(0, NSEQ, fetch, 0)
    head[...] = x[:BAND]
    tail[...] = x[SDEV - BAND :]


def place(received):
    return pl.pallas_call(
        place_kernel,
        out_shape=[jax.ShapeDtypeStruct((n, D), BF16) for n in (SDEV, BAND, BAND)],
        in_specs=[VMEM],
        out_specs=[VMEM] * 3,
        scratch_shapes=[
            pltpu.VMEM((NSEQ, 128), jnp.int32),
            pltpu.SMEM((NSEQ, 128), jnp.int32),
            dma(),
        ],
        compiler_params=pltpu.CompilerParams(vmem_limit_bytes=SMALL_VMEM),
        name="place_blocks",
    )(received)


def doc_bounds(info, doc_len, start):
    u0 = info[0] + LEAD + start
    doc = lax.shift_right_logical(u0, 13)
    base = doc * DOC_LEN
    length = doc_len[doc]
    low = jnp.maximum(0, LEAD - base)
    high = jnp.minimum(length, SPAN + LEAD - base)
    return u0 - base, length, low, high


def reach_table(info, doc_len, start):
    rel, _, low, high = doc_bounds(info, doc_len, start)
    j = iota((CH, WIN), 1)
    dist = jnp.abs(iota((CH, WIN), 0) + BAND - j)
    key = rel - BAND + j
    keep = (dist <= BAND) & (((key >= low) & (key < high)) | (dist == 0))
    return jnp.where(keep, -dist.astype(F32), FAR)


def layer_norm(v, gain, shift):
    centre = jnp.mean(v, axis=-1, keepdims=True)
    v = v - centre
    spread = jnp.mean(v * v, axis=-1, keepdims=True)
    return v * lax.rsqrt(spread + norm_eps) * gain + shift


def gelu(x):
    z = jnp.abs(x)
    t = 1.0 / (1.0 + z * (0.3275911 * math.sqrt(0.5)))
    p = t * (0.5 * 1.061405429) + (0.5 * -1.453152027)
    p = p * t + (0.5 * 1.421413741)
    p = p * t + (0.5 * -0.284496736)
    p = p * t + (0.5 * 0.254829592)
    q = p * t * jnp.exp2(x * x * (-0.5 * LOG2E))
    return jnp.maximum(x, 0.0) - z * q


def attend_pair(pair, chunks, qref, qrows, kvref, reach, slopes, att):
    lanes = pl.ds(pl.multiple_of(pair * 128, 128), 128)
    vlanes = pl.ds(pl.multiple_of(D + pair * 128, 128), 128)
    left = iota((CH, 128), 1) < 64
    ones = jnp.ones((WIN, 128), BF16)
    for n, c in enumerate(chunks):
        q = qref[pl.ds(qrows[n], CH), lanes]
        window = pl.ds(c * CH - kvref[1], WIN)
        k = kvref[0][window, lanes]
        v = jnp.concatenate([kvref[0][window, vlanes], ones], axis=1)
        halves = []
        for side in range(2):
            mine = left if side == 0 else jnp.logical_not(left)
            s = lax.dot_general(
                jnp.where(mine, q, jnp.zeros_like(q)),
                k,
                (((1,), (1,)), ((), ())),
                preferred_element_type=F32,
            )
            s = s + slopes[2 * pair + side] * reach[n]
            s = s - jnp.max(s, axis=-1, keepdims=True)
            o = dot(jnp.exp2(s).astype(BF16), v)
            halves.append(o[:, :128] / o[:, 128:])
        att[pl.ds(n * CH, CH), lanes] = jnp.where(left, halves[0], halves[1]).astype(BF16)


def pool_tile(info, doc_len, lists, chunk, enc, centroids):
    rel, length, _, _ = doc_bounds(info, doc_len, chunk * CH)
    r = iota((TROWS, CH), 0)
    i = iota((TROWS, CH), 1)
    scale = jnp.where(length - rel - 2 * r >= 2, 0.5, 1.0)
    mine = (lax.shift_right_logical(i, 1) == r) & (rel + i < length)
    pooled = dot(jnp.where(mine, scale, 0.0).astype(BF16), enc)
    pick = (iota((TROWS, centroids.shape[0]), 1) == lists[chunk]).astype(BF16)
    return (pooled - dot(pick, centroids[...])).astype(BF16)


def start_all(copies):
    for c in copies:
        c.start()


def wait_all(copies):
    for c in copies:
        c.wait()


def layer_of(chunks, att, x_rows, first, active, ws, loads, vecs):
    b_out, g1, s1, b_down, g2, s2 = vecs
    w_out, w_glu, w_down = ws
    loads[0].wait()
    mixed = dot(att[...], w_out[...]) + b_out[...] + x_rows.astype(F32)
    first[...] = layer_norm(mixed, g1[...], s1[...]).astype(BF16)
    loads[1].wait()

    def part(i, _):
        cols = pl.ds(pl.multiple_of(i * FC, FC), FC)
        up = pl.ds(pl.multiple_of(FF + i * FC, FC), FC)
        f = first[...]
        active[:, cols] = (gelu(dot(f, w_glu[:, cols])) * dot(f, w_glu[:, up])).astype(BF16)
        return 0

    lax.fori_loop(0, FF // FC, part, 0, unroll=FF_UNROLL)
    loads[2].wait()
    second = dot(active[...], w_down[...]) + b_down[...] + first[...].astype(F32)
    return layer_norm(second, g2[...], s2[...]).astype(BF16)


def loads_of(sources, targets, sems):
    return [pltpu.make_async_copy(s, t, sems.at[i]) for i, (s, t) in enumerate(zip(sources, targets))]


def mid_kernel(
    info, doc_len, lists, slopes, head,
    w_qkv_h, w_out_h, w_glu_h, w_down_h, x,
    b_qkv, b_out, g1, s1, b_down, g2, s2, centroids,
    enc_h, qs, kvs, tiles,
    w_qkv, w_out, w_glu, w_down, att, first, active, reach, enc, wsem, osem,
):
    chunks = (1, 2)
    ws = (w_out, w_glu, w_down)
    heads = pltpu.make_async_copy(w_qkv_h, w_qkv, wsem.at[3])
    heads.start()
    loads = loads_of((w_out_h, w_glu_h, w_down_h), ws, wsem)
    for n, c in enumerate(chunks):
        reach[n] = reach_table(info, doc_len, c * CH)
    heads.wait()
    start_all(loads)
    qs[...] = ((dot(x[...], w_qkv[:, :D]) + b_qkv[:, :D]) * (LOG2E / 8.0)).astype(BF16)
    kvs[...] = (dot(x[...], w_qkv[:, D:]) + b_qkv[:, D:]).astype(BF16)

    def pairs(pair, _):
        attend_pair(pair, chunks, qs, (CH, 2 * CH), (kvs, BAND), reach, slopes, att)
        return 0

    lax.fori_loop(0, H // 2, pairs, 0, unroll=PAIR_UNROLL)
    enc[...] = layer_of(
        chunks, att, x[pl.ds(CH, 2 * CH)], first, active, ws, loads,
        (b_out, g1, s1, b_down, g2, s2),
    )
    last = pltpu.make_async_copy(enc, enc_h.at[pl.ds(CH, 2 * CH)], osem.at[2])
    last.start()
    for n, c in enumerate(chunks):
        tiles[n] = pool_tile(info, doc_len, lists, c, enc[pl.ds(n * CH, CH)], centroids)
    last.wait()


def edge_kernel(
    chunk, info, doc_len, lists, slopes,
    enc_in, w_qkv_h, w_out_h, w_glu_h, w_down_h, halo, x, q, kv,
    b_qkv, b_out, g1, s1, b_down, g2, s2, centroids,
    *rest,
):
    enc_h, tile, kvs, w_kv, w_out, w_glu, w_down = rest[-14:-7]
    att, first, active, reach, enc, wsem, osem = rest[-7:]
    ws = (w_out, w_glu, w_down)
    sides_load = pltpu.make_async_copy(w_qkv_h.at[:, pl.ds(D, 2 * D)], w_kv, wsem.at[3])
    sides_load.start()
    loads = loads_of((w_out_h, w_glu_h, w_down_h), ws, wsem)
    start = chunk * CH
    reach[0] = reach_table(info, doc_len, start)
    sides_load.wait()
    start_all(loads)
    sides = (dot(halo[...], w_kv[...]) + b_qkv[:, D:]).astype(BF16)
    if chunk == 0:
        kvs[pl.ds(0, BAND)] = sides
        kvs[pl.ds(BAND, WIN - BAND)] = kv[pl.ds(0, WIN - BAND)]
    else:
        kvs[pl.ds(0, WIN - BAND)] = kv[pl.ds(start - BAND, WIN - BAND)]
        kvs[pl.ds(WIN - BAND, BAND)] = sides

    def pairs(pair, _):
        attend_pair(pair, (chunk,), q, (start,), (kvs, start), reach, slopes, att)
        return 0

    lax.fori_loop(0, H // 2, pairs, 0, unroll=PAIR_UNROLL)
    enc[...] = layer_of(
        (chunk,), att, x[pl.ds(start, CH)], first, active, ws, loads,
        (b_out, g1, s1, b_down, g2, s2),
    )
    last = pltpu.make_async_copy(enc, enc_h.at[pl.ds(start, CH)], osem.at[2])
    last.start()
    tile[...] = pool_tile(info, doc_len, lists, chunk, enc[...], centroids)
    last.wait()


def dma(*shape):
    return pltpu.SemaphoreType.DMA(shape)


def common_scratch(rows):
    return [
        pltpu.VMEM((D, D), BF16),
        pltpu.VMEM((D, 2 * FF), BF16),
        pltpu.VMEM((FF, D), BF16),
        pltpu.VMEM((rows, D), BF16),
        pltpu.VMEM((rows, D), BF16),
        pltpu.VMEM((rows, FF), BF16),
        pltpu.VMEM((rows // CH, CH, WIN), F32),
        pltpu.VMEM((rows, D), BF16),
        dma(4),
        dma(3),
    ]


def mid_layer(info, doc_len, lists, slopes, head, x, ws, vecs):
    return pl.pallas_call(
        mid_kernel,
        out_shape=(
            jax.ShapeDtypeStruct((SDEV, D), BF16),
            jax.ShapeDtypeStruct((SDEV, D), BF16),
            jax.ShapeDtypeStruct((SDEV, 2 * D), BF16),
            jax.ShapeDtypeStruct((2, TROWS, D), BF16),
        ),
        in_specs=[SMEM] * 4 + [ANY] * 5 + [VMEM] * 9,
        out_specs=(ANY, VMEM, VMEM, VMEM),
        scratch_shapes=[pltpu.VMEM((D, 3 * D), BF16)] + common_scratch(2 * CH),
        compiler_params=pltpu.CompilerParams(vmem_limit_bytes=KERNEL_VMEM),
        cost_estimate=pl.CostEstimate(
            flops=14_000_000_000, bytes_accessed=30_000_000, transcendentals=8_000_000
        ),
        name="mid_layer",
    )(info, doc_len, lists, slopes, head, *ws, x, *vecs)


def edge_layer(chunk, info, doc_len, lists, slopes, halo, x, q, kv, enc, ws, vecs, after=()):
    return pl.pallas_call(
        functools.partial(edge_kernel, chunk),
        out_shape=(
            jax.ShapeDtypeStruct((SDEV, D), BF16),
            jax.ShapeDtypeStruct((TROWS, D), BF16),
        ),
        in_specs=[SMEM] * 4 + [ANY] * 5 + [VMEM] * 12 + [ANY] * len(after),
        out_specs=(ANY, VMEM),
        input_output_aliases={4: 0},
        scratch_shapes=[pltpu.VMEM((WIN, 2 * D), BF16), pltpu.VMEM((D, 2 * D), BF16)]
        + common_scratch(CH),
        compiler_params=pltpu.CompilerParams(vmem_limit_bytes=KERNEL_VMEM),
        cost_estimate=pl.CostEstimate(
            flops=6_000_000_000, bytes_accessed=15_000_000, transcendentals=4_000_000
        ),
        name="edge_layer_%d" % chunk,
    )(info, doc_len, lists, slopes, enc, *ws, halo, x, q, kv, *vecs, *after)


def slot_of(here, lists, k, tile):
    device = (here[0] + BATCHES - k) & (BATCHES - 1)
    mine = [lax.shift_right_logical(lists[k * 4 + t], 6) == here[0] for t in range(4)]
    counts = [m.astype(jnp.int32) for m in mine]
    rank = sum(counts[:tile], jnp.int32(0))
    row = pl.multiple_of((device * CAP + jnp.minimum(rank, CAP - 1)) * TROWS, TROWS)
    return mine[tile], row, device, sum(counts, jnp.int32(0))


def store_kernel(here, lists, *refs):
    pairs, singles, out, sems = refs[:4], refs[4:8], refs[8], refs[9]
    moves = []
    for k in range(BATCHES):
        for t, source in ((1, pairs[k].at[0]), (2, pairs[k].at[1]), (0, singles[k])):
            mine, row, _, _ = slot_of(here, lists, k, t)
            dst = out.at[pl.ds(row, TROWS)]
            moves.append((mine, pltpu.make_async_copy(source, dst, sems.at[len(moves)])))
        _, _, device, total = slot_of(here, lists, k, 0)
        for r in range(CAP):

            @pl.when(total <= r)
            def _():
                row = pl.multiple_of((device * CAP + r) * TROWS, TROWS)
                out[pl.ds(row, TROWS)] = jnp.zeros((TROWS, D), BF16)

    for go, copy in moves:
        pl.when(go)(copy.start)
    for go, copy in moves:
        pl.when(go)(copy.wait)


def store(here, lists, pairs, singles):
    return pl.pallas_call(
        store_kernel,
        out_shape=jax.ShapeDtypeStruct((BATCHES * CAP * TROWS, D), BF16),
        in_specs=[SMEM] * 2 + [ANY] * 8,
        out_specs=VMEM,
        scratch_shapes=[dma(12)],
        compiler_params=pltpu.CompilerParams(vmem_limit_bytes=SMALL_VMEM),
        name="store_tiles",
    )(here, lists, *pairs, *singles)


def store_last_kernel(here, lists, *refs):
    singles, out, sems = refs[:4], refs[5], refs[6]
    moves = []
    for k in range(BATCHES):
        mine, row, _, _ = slot_of(here, lists, k, 3)
        dst = out.at[pl.ds(row, TROWS)]
        moves.append((mine, pltpu.make_async_copy(singles[k], dst, sems.at[k])))
    for go, copy in moves:
        pl.when(go)(copy.start)
    for go, copy in moves:
        pl.when(go)(copy.wait)


def store_last(here, lists, singles, stored):
    return pl.pallas_call(
        store_last_kernel,
        out_shape=jax.ShapeDtypeStruct(stored.shape, BF16),
        in_specs=[SMEM] * 2 + [VMEM] * 4 + [ANY],
        out_specs=ANY,
        input_output_aliases={6: 0},
        scratch_shapes=[dma(4)],
        compiler_params=pltpu.CompilerParams(vmem_limit_bytes=SMALL_VMEM),
        name="store_last_tile",
    )(here, lists, *singles, stored)


def on_device(
    packed, block_dest, doc_len, w_qkv, b_qkv, w_out, b_out, norm1_gain, norm1_shift,
    w_glu, w_down, b_down, norm2_gain, norm2_shift, centroids, tile_list,
):
    seq_here = lax.axis_index("seq")
    batch_here = lax.axis_index("batch")

    def from_batch(v):
        turns = [[(i, (i + k) % BATCHES) for i in range(BATCHES)] for k in range(1, BATCHES)]
        return [v] + [lax.ppermute(v, "batch", t) for t in turns]

    received = lax.all_to_all(
        pack(packed, block_dest), "seq", split_axis=0, concat_axis=0, tiled=True
    )
    lists = jnp.concatenate(from_batch(tile_list))
    info = (seq_here * SDEV).astype(jnp.int32).reshape(1)
    here = batch_here.astype(jnp.int32).reshape(1)
    slopes = jnp.asarray(head_slopes(H) * np.float32(LOG2E))
    row = lambda v: v.reshape(1, -1)
    ws = (w_qkv, w_out, w_glu, w_down)
    vecs = (
        row(b_qkv), row(b_out), row(norm1_gain), row(norm1_shift),
        row(b_down), row(norm2_gain), row(norm2_shift), centroids,
    )
    x, head, tail = place(received)
    up = [(i, i + 1) for i in range(NSEQ - 1)]
    down = [(j, i) for i, j in up]
    before = lax.ppermute(tail, "seq", up)
    after = lax.ppermute(head, "seq", down)
    enc, q, kv, pair = mid_layer(info, doc_len, lists, slopes, head, x, ws, vecs)
    pairs = from_batch(pair)
    enc, tile_0 = edge_layer(0, info, doc_len, lists, slopes, before, x, q, kv, enc, ws, vecs)
    firsts = from_batch(tile_0)
    enc, tile_3 = edge_layer(
        3, info, doc_len, lists, slopes, after, x, q, kv, enc, ws, vecs, after=pairs[1:]
    )
    tile_3, *firsts = lax.optimization_barrier((tile_3, *firsts))
    lasts = from_batch(tile_3)
    stored = store(here, lists, pairs, firsts)
    stored = store_last(here, lists, lasts, stored)
    return enc, stored.reshape(1, 1, BATCHES * CAP * TROWS, D)


def solution(mesh):
    return jax.shard_map(
        on_device,
        mesh=mesh,
        in_specs=(
            P(("batch", "seq"), None),
            P(("batch", "seq")),
            P("batch"),
            P(), P(), P(), P(), P(), P(), P(), P(), P(), P(), P(), P(),
            P(("batch", "seq")),
        ),
        out_specs=(P(("batch", "seq"), None), P("batch", "seq", None, None)),
        check_vma=False,
    )
```

time: 316 us -> 152 us (0.48)
  the two profiles are of different devices: /device:TPU:18 before, /device:TPU:1 now
where the time goes in v1:
time: 152 us; the launch traced here: 149 us
  Pallas kernels  69.6 us (46%)
  waiting for transfers between devices  40 us (26%)
  starting transfers between devices  33.9 us (22%)
  local copies, waits for them, and re-layouts  3.83 us (3%)
    pallas_call x2, Pallas kernels, edge_layer(): pl.pallas_call(functools.partial(edge_kernel, chunk), out_shape=(jax.Shap...  33 us
    all_to_all x1, waiting for transfers between devices, on_device(): lax.all_to_all(pack(packed, block_dest), 'seq', split_axis=0, concat_axis...  32.7 us
    pallas_call x1, Pallas kernels, mid_layer(): pl.pallas_call(mid_kernel, out_shape=(jax.ShapeDtypeStruct((SDEV, D), BF1...  29.1 us
    ppermute x12, starting transfers between devices, from_batch(): return [v] + [lax.ppermute(v, 'batch', t) for t in turns]  18.1 us
    all_to_all x1, starting transfers between devices, on_device(): lax.all_to_all(pack(packed, block_dest), 'seq', split_axis=0, concat_axis...  8.73 us
    ppermute x12, waiting for transfers between devices, from_batch(): return [v] + [lax.ppermute(v, 'batch', t) for t in turns]  7.29 us
    ppermute x1, starting transfers between devices, on_device(): before = lax.ppermute(tail, 'seq', up)  4.17 us
    unnamed x32, local copies, waits for them, and re-layouts  3.79 us
  transfers between devices with their start and end apart: 15, of which 6 were waited for; matrix products, arithmetic and copies ran while one was open for 0% of the time, Pallas kernels for 44%

profile of v1, /device:TPU:1, one launch (start us, length us, event | category | flops | bytes accessed | tf_op | source)
XLA Modules:
  0.0 148.6 jit_solution(14918635859780503861)
XLA Ops:
  0.6 1.4 copy-done.4
  2.0 0.7 copy-done.7
  2.7 1.4 pack_blocks.1
  4.1 0.0 copy-start
  4.1 1.7 %copy-done = bf16[32,400,128]{2,1,0:T(8,128)(2,1)} copy-done((bf16[32,400,128]{2,1,0:T(8,128)(2,1)}, bf16[32,400,128]{2,1,0:T(8,128)(2,1)S(1)}, u32[]{:S(2)}) %copy-start) | copy-done | bytes 3276824
  5.8 0.0 copy-start.11
  5.8 0.0 copy-start.12
  5.9 0.0 copy-start.13
  5.9 0.0 copy-start.14
  5.9 8.7 %all-to-all-start = ((bf16[32,400,128]{2,1,0:T(8,128)(2,1)}), bf16[32,400,128]{2,1,0:T(8,128)(2,1)S(1)}, u32[]{:S(2)}, u32[]{:S(2)}) async-start(bf16[32,400,128]{2,1,0:T(8,128)(2,1)} %copy-done), calls=%async_computation | async-start | bytes 6553600 | tf_op jit(solution)/shard_map/all_to_all | solution.py:467
  14.6 0.0 copy-done.15
  14.6 1.7 %collective-permute-start = (s32[4]{0:T(128)S(1)}, s32[4]{0:T(128)S(1)}, u32[]{:S(2)}, u32[]{:S(2)}) collective-permute-start(s32[4]{0:T(128)S(1)} %copy-done.15), channel_id=1, source_target_pairs={{0,32},{32,64},{64,96},{96,0},{1,33},{33,65},{65,97},{97,1},{2,34}... | collective-permute-start | bytes 56 | tf_op jit(solution)/shard_map/ppermute | solution.py:465
  16.3 3.3 %collective-permute-start.1 = (s32[4]{0:T(128)S(1)}, s32[4]{0:T(128)S(1)}, u32[]{:S(2)}, u32[]{:S(2)}) collective-permute-start(s32[4]{0:T(128)S(1)} %copy-done.15), channel_id=1, source_target_pairs={{0,64},{32,96},{64,0},{96,32},{1,65},{33,97},{65,1},{97,33},{2,66}... | collective-permute-start | bytes 56 | tf_op jit(solution)/shard_map/ppermute | solution.py:465
  19.6 0.7 collective-permute-start.2
  20.5 0.0 collective-permute-done
  20.5 0.3 collective-permute-done.1
  20.9 1.5 collective-permute-done.2
  22.3 0.1 pad_add_fusion.lists
  22.4 32.7 %all-to-all-done.received = bf16[32,400,128]{2,1,0:T(8,128)(2,1)S(1)} async-done(((bf16[32,400,128]{2,1,0:T(8,128)(2,1)}), bf16[32,400,128]{2,1,0:T(8,128)(2,1)S(1)}, u32[]{:S(2)}, u32[]{:S(2)}) %all-to-all-start) | async-done | bytes 3276832 | tf_op jit(solution)/shard_map/all_to_all | solution.py:467
  55.1 1.9 %place_blocks.1 = (bf16[1024,768]{1,0:T(8,128)(2,1)S(1)}, bf16[256,768]{1,0:T(8,128)(2,1)S(1)}, bf16[256,768]{1,0:T(8,128)(2,1)S(1)}) custom-call(bf16[32,400,128]{2,1,0:T(8,128)(2,1)S(1)} %all-to-all-done.received), custom_call_target="tpu_custom_call" | custom-call | tf_op jit(solution)/shard_map/place_blocks/pallas_call | solution.py:130
  57.0 4.2 %collective-permute-start.3 = (bf16[256,768]{1,0:T(8,128)(2,1)S(1)}, bf16[256,768]{1,0:T(8,128)(2,1)S(1)}, u32[]{:S(2)}, u32[]{:S(2)}) collective-permute-start(bf16[256,768]{1,0:T(8,128)(2,1)S(1)} %get-tuple-element.21), channel_id=1, source_target_pairs={{0,1},{1,2},{2,3},{3,4},{4,5},{5,6},{6,7},{7,8},{8,9},{9,10},{10,1... | collective-permute-start | bytes 1179656 | tf_op jit(solution)/shard_map/ppermute | solution.py:483
  61.2 29.1 %mid_layer.1 = (bf16[1024,768]{1,0:T(8,128)(2,1)}, bf16[1024,768]{1,0:T(8,128)(2,1)S(1)}, bf16[1024,1536]{1,0:T(8,128)(2,1)}, bf16[2,128,768]{2,1,0:T(8,128)(2,1)S(1)}) custom-call(s32[1]{0:T(128)} %bitcast.info, s32[5]{0:T(128)S(1)} %copy-done.5, s32[16]{0:T(128)S(1)} %pad_add_fusion.lists, f32[12]{0:T(128)S(1)} %copy-done.6, ...), custom_call_target="tpu_custom_call" | custom-call | flops 14000000000 | bytes 30000000 | tf_op jit(solution)/shard_map/mid_layer/pallas_call | solution.py:348
  90.3 0.0 copy-start.1
  90.4 1.7 %collective-permute-start.5 = (bf16[2,128,768]{2,1,0:T(8,128)(2,1)S(1)}, bf16[2,128,768]{2,1,0:T(8,128)(2,1)S(1)}, u32[]{:S(2)}, u32[]{:S(2)}) collective-permute-start(bf16[2,128,768]{2,1,0:T(8,128)(2,1)S(1)} %get-tuple-element.25.refs_0_), channel_id=1, source_target_pairs={{0,32},{32,64},{64,96},{96,0},{1,33},{33,65},{65,97},{97,1},{2,34}... | collective-permute-start | bytes 1179656 | tf_op jit(solution)/shard_map/ppermute | solution.py:465
  92.1 3.3 %collective-permute-start.6 = (bf16[2,128,768]{2,1,0:T(8,128)(2,1)S(1)}, bf16[2,128,768]{2,1,0:T(8,128)(2,1)S(1)}, u32[]{:S(2)}, u32[]{:S(2)}) collective-permute-start(bf16[2,128,768]{2,1,0:T(8,128)(2,1)S(1)} %get-tuple-element.25.refs_0_), channel_id=1, source_target_pairs={{0,64},{32,96},{64,0},{96,32},{1,65},{33,97},{65,1},{97,33},{2,66}... | collective-permute-start | bytes 1179656 | tf_op jit(solution)/shard_map/ppermute | solution.py:465
  95.4 0.7 collective-permute-start.7
  96.1 2.9 %collective-permute-start.4 = (bf16[256,768]{1,0:T(8,128)(2,1)S(1)}, bf16[256,768]{1,0:T(8,128)(2,1)S(1)}, u32[]{:S(2)}, u32[]{:S(2)}) collective-permute-start(bf16[256,768]{1,0:T(8,128)(2,1)S(1)} %get-tuple-element.18.head), channel_id=1, source_target_pairs={{1,0},{2,1},{3,2},{4,3},{5,4},{6,5},{7,6},{8,7},{9,8},{10,9},{11,1... | collective-permute-start | bytes 1179656 | tf_op jit(solution)/shard_map/ppermute | solution.py:484
  99.0 0.0 collective-permute-done.3.halo
  99.0 17.1 %edge_layer_0.1 = (bf16[1024,768]{1,0:T(8,128)(2,1)}, bf16[128,768]{1,0:T(8,128)(2,1)S(1)}) custom-call(s32[1]{0:T(128)} %bitcast.info, s32[5]{0:T(128)S(1)} %copy-done.5, s32[16]{0:T(128)S(1)} %pad_add_fusion.lists, f32[12]{0:T(128)S(1)} %copy-done.6, bf16[1024,768]{1,0:T(8,128)(2,1)} %get-tuple-element.20.enc_in, ...), custom_call_target="tpu_custom_call", output_to_operand_aliasing={{0}: (4, {})} | custom-call | flops 6000000000 | bytes 15000000 | tf_op jit(solution)/shard_map/edge_layer_0/pallas_call | solution.py:368
  116.1 0.1 collective-permute-start.10
  116.2 0.0 collective-permute-done.5.rest_0_.refs_1_
  116.2 1.4 collective-permute-start.8
  117.6 0.0 collective-permute-done.6.rest_1_.refs_2_
  117.6 1.1 collective-permute-start.9
  118.8 0.0 collective-permute-done.7.rest_2_.refs_3_
  118.8 0.0 collective-permute-done.4.halo
  118.8 15.9 %edge_layer_3.1 = (bf16[1024,768]{1,0:T(8,128)(2,1)}, bf16[128,768]{1,0:T(8,128)(2,1)S(1)}) custom-call(s32[1]{0:T(128)} %bitcast.info, s32[5]{0:T(128)S(1)} %copy-done.5, s32[16]{0:T(128)S(1)} %pad_add_fusion.lists, f32[12]{0:T(128)S(1)} %copy-done.6, bf16[1024,768]{1,0:T(8,128)(2,1)} %get-tuple-element.24.enc_in, ...), custom_call_target="tpu_custom_call", output_to_operand_aliasing={{0}: (4, {})} | custom-call | flops 6000000000 | bytes 15000000 | tf_op jit(solution)/shard_map/edge_layer_3/pallas_call | solution.py:368
  134.7 0.0 collective-permute-done.10.refs_7_
  134.7 0.0 collective-permute-done.8.refs_5_
  134.7 0.0 collective-permute-done.9.refs_6_
  134.8 0.8 collective-permute-start.11
  135.6 2.4 %collective-permute-start.12 = (bf16[128,768]{1,0:T(8,128)(2,1)S(1)}, bf16[128,768]{1,0:T(8,128)(2,1)S(1)}, u32[]{:S(2)}, u32[]{:S(2)}) collective-permute-start(bf16[128,768]{1,0:T(8,128)(2,1)S(1)} %get-tuple-element.29.refs_0_), channel_id=1, source_target_pairs={{0,64},{32,96},{64,0},{96,32},{1,65},{33,97},{65,1},{97,33},{2,66}... | collective-permute-start | bytes 589832 | tf_op jit(solution)/shard_map/ppermute | solution.py:465
  138.0 0.8 collective-permute-start.13
  138.8 2.9 %store_tiles.1.refs_4_ = bf16[1024,768]{1,0:T(8,128)(2,1)} custom-call(s32[1]{0:T(128)} %bitcast.1.here, s32[16]{0:T(128)S(1)} %pad_add_fusion.lists, bf16[2,128,768]{2,1,0:T(8,128)(2,1)S(1)} %get-tuple-element.25.refs_0_, bf16[2,128,768]{2,1,0:T(8,128)(2,1)S(1)} %collective-permute-done.5.rest_0_.refs_1_, ...), custom_call_target="tpu_custom_call" | custom-call | tf_op jit(solution)/shard_map/store_tiles/pallas_call | solution.py:419
  141.7 1.0 collective-permute-done.11.refs_1_
  142.6 4.4 %collective-permute-done.12.refs_2_ = bf16[128,768]{1,0:T(8,128)(2,1)S(1)} collective-permute-done((bf16[128,768]{1,0:T(8,128)(2,1)S(1)}, bf16[128,768]{1,0:T(8,128)(2,1)S(1)}, u32[]{:S(2)}, u32[]{:S(2)}) %collective-permute-start.12) | collective-permute-done | bytes 196640 | tf_op jit(solution)/shard_map/ppermute | solution.py:465
  147.0 0.1 collective-permute-done.13.refs_3_
  147.1 1.3 store_last_tile.1
  (29 shorter events, 0.1 us)
Async XLA Ops:
  0.6 1.4 copy-start.4
  2.0 0.7 copy-start.7
  4.1 1.7 %copy-start = (bf16[32,400,128]{2,1,0:T(8,128)(2,1)}, bf16[32,400,128]{2,1,0:T(8,128)(2,1)S(1)}, u32[]{:S(2)}) copy-start(bf16[32,400,128]{2,1,0:T(8,128)(2,1)S(1)} %pack_blocks.1) | copy-start | bytes 9830404
  5.8 8.8 %copy-start.15 = (s32[4]{0:T(128)S(1)}, s32[4]{0:T(128)}, u32[]{:S(2)}) copy-start(s32[4]{0:T(128)} %param.32) | copy-start | bytes 52
  5.8 14.5 %copy-start.8 = (f32[2304]{0:T(1024)S(1)}, f32[2304]{0:T(1024)}, u32[]{:S(2)}) copy-start(f32[2304]{0:T(1024)} %param.21) | copy-start | bytes 27652
  5.8 14.6 %copy-start.9 = (f32[768]{0:T(1024)S(1)}, f32[768]{0:T(1024)}, u32[]{:S(2)}) copy-start(f32[768]{0:T(1024)} %param.23) | copy-start | bytes 9220
  5.8 14.6 %copy-start.10 = (f32[768]{0:T(1024)S(1)}, f32[768]{0:T(1024)}, u32[]{:S(2)}) copy-start(f32[768]{0:T(1024)} %param.24) | copy-start | bytes 9220
  5.8 14.6 %copy-start.11 = (f32[768]{0:T(1024)S(1)}, f32[768]{0:T(1024)}, u32[]{:S(2)}) copy-start(f32[768]{0:T(1024)} %param.25) | copy-start | bytes 9220
  5.8 14.6 %copy-start.12 = (f32[768]{0:T(1024)S(1)}, f32[768]{0:T(1024)}, u32[]{:S(2)}) copy-start(f32[768]{0:T(1024)} %param.28) | copy-start | bytes 9220
  5.9 14.6 %copy-start.13 = (f32[768]{0:T(1024)S(1)}, f32[768]{0:T(1024)}, u32[]{:S(2)}) copy-start(f32[768]{0:T(1024)} %param.29) | copy-start | bytes 9220
  5.9 14.6 %copy-start.14 = (f32[768]{0:T(1024)S(1)}, f32[768]{0:T(1024)}, u32[]{:S(2)}) copy-start(f32[768]{0:T(1024)} %param.30) | copy-start | bytes 9220
  5.9 49.2 %all-to-all-start = ((bf16[32,400,128]{2,1,0:T(8,128)(2,1)}), bf16[32,400,128]{2,1,0:T(8,128)(2,1)S(1)}, u32[]{:S(2)}, u32[]{:S(2)}) async-start(bf16[32,400,128]{2,1,0:T(8,128)(2,1)} %copy-done), calls=%async_computation | async-start | bytes 6553600 | tf_op jit(solution)/shard_map/all_to_all | solution.py:467
  14.6 5.9 %collective-permute-start = (s32[4]{0:T(128)S(1)}, s32[4]{0:T(128)S(1)}, u32[]{:S(2)}, u32[]{:S(2)}) collective-permute-start(s32[4]{0:T(128)S(1)} %copy-done.15), channel_id=1, source_target_pairs={{0,32},{32,64},{64,96},{96,0},{1,33},{33,65},{65,97},{97,1},{2,34}... | collective-permute-start | bytes 56 | tf_op jit(solution)/shard_map/ppermute | solution.py:465
  16.3 4.5 %collective-permute-start.1 = (s32[4]{0:T(128)S(1)}, s32[4]{0:T(128)S(1)}, u32[]{:S(2)}, u32[]{:S(2)}) collective-permute-start(s32[4]{0:T(128)S(1)} %copy-done.15), channel_id=1, source_target_pairs={{0,64},{32,96},{64,0},{96,32},{1,65},{33,97},{65,1},{97,33},{2,66}... | collective-permute-start | bytes 56 | tf_op jit(solution)/shard_map/ppermute | solution.py:465
  19.6 2.7 %collective-permute-start.2 = (s32[4]{0:T(128)S(1)}, s32[4]{0:T(128)S(1)}, u32[]{:S(2)}, u32[]{:S(2)}) collective-permute-start(s32[4]{0:T(128)S(1)} %copy-done.15), channel_id=1, source_target_pairs={{0,96},{32,0},{64,32},{96,64},{1,97},{33,1},{65,33},{97,65},{2,98}... | collective-permute-start | bytes 56 | tf_op jit(solution)/shard_map/ppermute | solution.py:465
  22.4 38.8 %copy-start.5 = (s32[5]{0:T(128)S(1)}, s32[5]{0:T(128)}, u32[]{:S(2)}) copy-start(s32[5]{0:T(128)} %doc_len.5) | copy-start | bytes 64
  22.4 38.8 %copy-start.6 = (f32[12]{0:T(128)S(1)}, f32[12]{0:T(128)}, u32[]{:S(2)}) copy-start(f32[12]{0:T(128)} %constant.13.clone.slopes) | copy-start | bytes 148
  55.1 6.1 %copy-start.2 = (bf16[768,768]{1,0:T(8,128)(2,1)S(1)}, bf16[768,768]{1,0:T(8,128)(2,1)}, u32[]{:S(2)}) copy-start(bf16[768,768]{1,0:T(8,128)(2,1)} %w_out_h.5) | copy-start | bytes 3538948
  55.1 6.1 %copy-start.3 = (bf16[256,768]{1,0:T(8,128)(2,1)S(1)}, bf16[256,768]{1,0:T(8,128)(2,1)}, u32[]{:S(2)}) copy-start(bf16[256,768]{1,0:T(8,128)(2,1)} %centroids.5) | copy-start | bytes 1179652
  57.0 42.0 %collective-permute-start.3 = (bf16[256,768]{1,0:T(8,128)(2,1)S(1)}, bf16[256,768]{1,0:T(8,128)(2,1)S(1)}, u32[]{:S(2)}, u32[]{:S(2)}) collective-permute-start(bf16[256,768]{1,0:T(8,128)(2,1)S(1)} %get-tuple-element.21), channel_id=1, source_target_pairs={{0,1},{1,2},{2,3},{3,4},{4,5},{5,6},{6,7},{7,8},{8,9},{9,10},{10,1... | collective-permute-start | bytes 1179656 | tf_op jit(solution)/shard_map/ppermute | solution.py:483
  90.3 25.7 %copy-start.1 = (bf16[1024,768]{1,0:T(8,128)(2,1)}, bf16[1024,768]{1,0:T(8,128)(2,1)S(1)}, u32[]{:S(2)}) copy-start(bf16[1024,768]{1,0:T(8,128)(2,1)S(1)} %get-tuple-element.22.q) | copy-start | bytes 4718596
  90.4 25.8 %collective-permute-start.5 = (bf16[2,128,768]{2,1,0:T(8,128)(2,1)S(1)}, bf16[2,128,768]{2,1,0:T(8,128)(2,1)S(1)}, u32[]{:S(2)}, u32[]{:S(2)}) collective-permute-start(bf16[2,128,768]{2,1,0:T(8,128)(2,1)S(1)} %get-tuple-element.25.refs_0_), channel_id=1, source_target_pairs={{0,32},{32,64},{64,96},{96,0},{1,33},{33,65},{65,97},{97,1},{2,34}... | collective-permute-start | bytes 1179656 | tf_op jit(solution)/shard_map/ppermute | solution.py:465
  92.1 25.6 %collective-permute-start.6 = (bf16[2,128,768]{2,1,0:T(8,128)(2,1)S(1)}, bf16[2,128,768]{2,1,0:T(8,128)(2,1)S(1)}, u32[]{:S(2)}, u32[]{:S(2)}) collective-permute-start(bf16[2,128,768]{2,1,0:T(8,128)(2,1)S(1)} %get-tuple-element.25.refs_0_), channel_id=1, source_target_pairs={{0,64},{32,96},{64,0},{96,32},{1,65},{33,97},{65,1},{97,33},{2,66}... | collective-permute-start | bytes 1179656 | tf_op jit(solution)/shard_map/ppermute | solution.py:465
  95.4 23.4 %collective-permute-start.7 = (bf16[2,128,768]{2,1,0:T(8,128)(2,1)S(1)}, bf16[2,128,768]{2,1,0:T(8,128)(2,1)S(1)}, u32[]{:S(2)}, u32[]{:S(2)}) collective-permute-start(bf16[2,128,768]{2,1,0:T(8,128)(2,1)S(1)} %get-tuple-element.25.refs_0_), channel_id=1, source_target_pairs={{0,96},{32,0},{64,32},{96,64},{1,97},{33,1},{65,33},{97,65},{2,98}... | collective-permute-start | bytes 1179656 | tf_op jit(solution)/shard_map/ppermute | solution.py:465
  96.1 22.7 %collective-permute-start.4 = (bf16[256,768]{1,0:T(8,128)(2,1)S(1)}, bf16[256,768]{1,0:T(8,128)(2,1)S(1)}, u32[]{:S(2)}, u32[]{:S(2)}) collective-permute-start(bf16[256,768]{1,0:T(8,128)(2,1)S(1)} %get-tuple-element.18.head), channel_id=1, source_target_pairs={{1,0},{2,1},{3,2},{4,3},{5,4},{6,5},{7,6},{8,7},{9,8},{10,9},{11,1... | collective-permute-start | bytes 1179656 | tf_op jit(solution)/shard_map/ppermute | solution.py:484
  116.1 18.6 %collective-permute-start.10 = (bf16[128,768]{1,0:T(8,128)(2,1)S(1)}, bf16[128,768]{1,0:T(8,128)(2,1)S(1)}, u32[]{:S(2)}, u32[]{:S(2)}) collective-permute-start(bf16[128,768]{1,0:T(8,128)(2,1)S(1)} %get-tuple-element.30.refs_4_), channel_id=1, source_target_pairs={{0,96},{32,0},{64,32},{96,64},{1,97},{33,1},{65,33},{97,65},{2,98}... | collective-permute-start | bytes 589832 | tf_op jit(solution)/shard_map/ppermute | solution.py:465
  116.2 18.6 %collective-permute-start.8 = (bf16[128,768]{1,0:T(8,128)(2,1)S(1)}, bf16[128,768]{1,0:T(8,128)(2,1)S(1)}, u32[]{:S(2)}, u32[]{:S(2)}) collective-permute-start(bf16[128,768]{1,0:T(8,128)(2,1)S(1)} %get-tuple-element.30.refs_4_), channel_id=1, source_target_pairs={{0,32},{32,64},{64,96},{96,0},{1,33},{33,65},{65,97},{97,1},{2,34}... | collective-permute-start | bytes 589832 | tf_op jit(solution)/shard_map/ppermute | solution.py:465
  117.6 17.1 %collective-permute-start.9 = (bf16[128,768]{1,0:T(8,128)(2,1)S(1)}, bf16[128,768]{1,0:T(8,128)(2,1)S(1)}, u32[]{:S(2)}, u32[]{:S(2)}) collective-permute-start(bf16[128,768]{1,0:T(8,128)(2,1)S(1)} %get-tuple-element.30.refs_4_), channel_id=1, source_target_pairs={{0,64},{32,96},{64,0},{96,32},{1,65},{33,97},{65,1},{97,33},{2,66}... | collective-permute-start | bytes 589832 | tf_op jit(solution)/shard_map/ppermute | solution.py:465
  134.8 7.9 %collective-permute-start.11 = (bf16[128,768]{1,0:T(8,128)(2,1)S(1)}, bf16[128,768]{1,0:T(8,128)(2,1)S(1)}, u32[]{:S(2)}, u32[]{:S(2)}) collective-permute-start(bf16[128,768]{1,0:T(8,128)(2,1)S(1)} %get-tuple-element.29.refs_0_), channel_id=1, source_target_pairs={{0,32},{32,64},{64,96},{96,0},{1,33},{33,65},{65,97},{97,1},{2,34}... | collective-permute-start | bytes 589832 | tf_op jit(solution)/shard_map/ppermute | solution.py:465
  135.6 11.5 %collective-permute-start.12 = (bf16[128,768]{1,0:T(8,128)(2,1)S(1)}, bf16[128,768]{1,0:T(8,128)(2,1)S(1)}, u32[]{:S(2)}, u32[]{:S(2)}) collective-permute-start(bf16[128,768]{1,0:T(8,128)(2,1)S(1)} %get-tuple-element.29.refs_0_), channel_id=1, source_target_pairs={{0,64},{32,96},{64,0},{96,32},{1,65},{33,97},{65,1},{97,33},{2,66}... | collective-permute-start | bytes 589832 | tf_op jit(solution)/shard_map/ppermute | solution.py:465
  138.0 9.1 %collective-permute-start.13 = (bf16[128,768]{1,0:T(8,128)(2,1)S(1)}, bf16[128,768]{1,0:T(8,128)(2,1)S(1)}, u32[]{:S(2)}, u32[]{:S(2)}) collective-permute-start(bf16[128,768]{1,0:T(8,128)(2,1)S(1)} %get-tuple-element.29.refs_0_), channel_id=1, source_target_pairs={{0,96},{32,0},{64,32},{96,64},{1,97},{33,1},{65,33},{97,65},{2,98}... | collective-permute-start | bytes 589832 | tf_op jit(solution)/shard_map/ppermute | solution.py:465
